TPU v7x, 256 devices: a whole 4x4x8 slice. The times are simulated.
256 devices in a mesh: dp: 16 (over z, y_hi), fsdp: 16 (over y_lo, x, core).
Axes of the slice: x: 4, y: 4 (y_hi: 2, y_lo: 2; y = y_hi * 2 + y_lo), z: 8, core: 2. Of those that a mesh axis runs over, the one named last changes fastest.
Arguments:
- activations: bfloat16 [131072, 4096], P(('dp', 'fsdp')), may hold values from -6 to 6
- cotangent: bfloat16 [131072, 4096], P(('dp', 'fsdp')), may hold values from -0.0625 to 0.0625
- basis: bfloat16 [4096, 1024], P('fsdp'), may hold values from -0.09375 to 0.09375
- weight: bfloat16 [4096, 4096], P(None, 'fsdp'), may hold values from -6 to 6
- first: float32 [1024, 16, 16, 16], P(None, 'fsdp', 'dp'), may hold values from -6 to 6
- second: float32 [1024, 16, 16, 16], P(None, 'fsdp', 'dp'), may hold values from 0.25 to 4
Outputs:
- new_weight: bfloat16 [4096, 4096], P(None, 'fsdp')
- new_first: float32 [1024, 16, 16, 16], P(None, 'fsdp', 'dp')
- new_second: float32 [1024, 16, 16, 16], P(None, 'fsdp', 'dp')
All inputs are finite; a program needn't handle non-finite values.
Results may differ from a plain program's by a relative error of at most 0.0045.
Values may be sent and summed in bfloat16 or wider, within the bound.
No kernel may reach another device: no remote copies, remote signals or barrier semaphores. Data moves between devices by JAX's collectives and lax.ppermute only.
A program may use at most 128 MiB of HBM per device.

v0:
```python
import math

import jax
import jax.numpy as jnp
from jax import lax
from jax.sharding import PartitionSpec as P

beta_one = 0.9
beta_two = 0.999
corr_one = 1.0 - math.exp(1000.0 * math.log(0.9))
corr_two = 1.0 - math.exp(1000.0 * math.log(0.999))
epsilon = 1e-08
rate = 0.5


def body(activations, cotangent, basis, weight, first, second):
    low_rank = basis.shape[1]
    width = activations.shape[1]
    fsdp_count = lax.axis_size("fsdp")
    dp_count = lax.axis_size("dp")
    owned = width // (fsdp_count * dp_count)
    projected = jnp.dot(
        activations,
        lax.all_gather(basis, "fsdp", axis=0, tiled=True),
        preferred_element_type=jnp.float32,
    )
    projected = projected.astype(jnp.bfloat16)
    gradient = lax.dot_general(
        projected, cotangent, (((0,), (0,)), ((), ())), preferred_element_type=jnp.float32
    )
    grouped = gradient.reshape(low_rank, fsdp_count, dp_count, owned)
    partial_sum = lax.psum_scatter(
        grouped.astype(jnp.bfloat16), "fsdp", scatter_dimension=1, tiled=True
    )
    summed = lax.psum_scatter(partial_sum, "dp", scatter_dimension=2, tiled=True).astype(
        jnp.float32
    )
    moment_one = beta_one * first + (1.0 - beta_one) * summed
    moment_two = beta_two * second + (1.0 - beta_two) * summed * summed
    update = moment_one / corr_one / (jnp.sqrt(moment_two / corr_two) + epsilon)
    update = update.astype(jnp.bfloat16).reshape(low_rank, owned)
    expanded = jnp.dot(
        lax.all_gather(basis, "fsdp", axis=0, tiled=True),
        update,
        preferred_element_type=jnp.float32,
    )
    replica = lax.axis_index("dp")
    current = lax.dynamic_slice_in_dim(weight, replica * owned, owned, 1)
    fresh = (current.astype(jnp.float32) - rate * expanded).astype(jnp.bfloat16)
    new_weight = lax.all_gather(fresh, "dp", axis=1, tiled=True)
    return (new_weight, moment_one, moment_two)


def solution(mesh):
    in_specs = (
        P(("dp", "fsdp"), None),
        P(("dp", "fsdp"), None),
        P("fsdp", None),
        P(None, "fsdp"),
        P(None, "fsdp", "dp", None),
        P(None, "fsdp", "dp", None),
    )
    out_specs = (P(None, "fsdp"), P(None, "fsdp", "dp", None), P(None, "fsdp", "dp", None))
    return jax.shard_map(body, mesh=mesh, in_specs=in_specs, out_specs=out_specs, check_vma=False)
```

profile of v0, /device:TPU:8, one launch (start us, length us, event | category | flops | bytes accessed | tf_op | source)
XLA Modules:
  0.0 477.4 jit_solution(3676903847617488819)
XLA Ops:
  7.2 0.0 copy-start
  7.2 0.0 all-gather.3.cloned.1.call-start
  7.2 0.7 all-gather.3.cloned.1.call-update
  7.9 0.0 reduce-scatter.3.cloned.1.call-start
  8.0 59.5 %all-gather.3.cloned.1.call-done = bf16[4096,1024]{1,0:T(8,128)(2,1)} async-done(((bf16[256,1024]{1,0:T(8,128)(2,1)}), bf16[4096,1024]{1,0:T(8,128)(2,1)}) %all-gather.3.cloned.1.call-update) | async-done | bytes 8388624 | tf_op jit(solution)/shard_map/all_gather | solution.py:43
  67.4 16.0 %convolution_convert_fusion = bf16[1024,4096]{1,0:T(8,128)(2,1)} fusion(bf16[512,4096]{1,0:T(8,128)(2,1)} %param.7, bf16[512,4096]{1,0:T(8,128)(2,1)} %param.6, bf16[4096,1024]{1,0:T(8,128)(2,1)} %all-gather.3.cloned.1.call-done), kind=kOutput, calls=%fused_computation | convolution fusion | flops 8594653184 | bytes 25165824 | tf_op jit(solution)/shard_map/dot_general | solution.py:28
  83.4 11.9 %copy.13 = bf16[1024,4096]{0,1:T(8,128)(2,1)} copy(bf16[1024,4096]{1,0:T(8,128)(2,1)} %convolution_convert_fusion) | data formatting | bytes 16777216 | tf_op jit(solution)/shard_map/convert_element_type | solution.py:33
  95.3 0.0 copy-start.3
  95.3 0.0 copy-start.4
  95.3 0.0 reduce-scatter.3.cloned.1.call-update
  95.4 0.0 reduce-scatter.5.cloned.1.call-start
  95.4 77.4 %reduce-scatter.3.cloned.1.call-done = bf16[1024,1,16,16]{0,3,2,1:T(8,128)(2,1)} async-done(((bf16[1024,16,16,16]{0,3,2,1:T(8,128)(2,1)}), bf16[1024,1,16,16]{0,3,2,1:T(8,128)(2,1)}) %reduce-scatter.3.cloned.1.call-update) | async-done | bytes 524304 | tf_op jit(solution)/shard_map/reduce_scatter | solution.py:32
  172.8 0.0 reduce-scatter.5.cloned.1.call-update
  172.8 0.0 all-gather.5.cloned.1.call-start
  172.9 0.0 copy-done
  172.9 0.4 constant_dynamic-slice_fusion
  173.3 0.3 copy.15
  173.6 202.5 %reduce-scatter.5.cloned.1.call-done = bf16[1024,1,1,16]{0,3,2,1:T(8,128)(2,1)} async-done(((bf16[1024,1,16,16]{0,3,2,1:T(8,128)(2,1)}), bf16[1024,1,1,16]{0,3,2,1:T(8,128)(2,1)}) %reduce-scatter.5.cloned.1.call-update) | async-done | bytes 32784 | tf_op jit(solution)/shard_map/reduce_scatter | solution.py:35
  376.0 0.0 copy-done.3
  376.1 0.0 copy-done.4
  376.1 0.8 fusion.4
  376.8 0.0 copy-start.1
  376.8 0.0 copy-start.2
  376.9 6.4 %fusion.2 = bf16[4096,16]{0,1:T(8,128)(2,1)} fusion(bf16[4096,1024]{1,0:T(8,128)(2,1)} %all-gather.3.cloned.1.call-done, bf16[4096,16]{0,1:T(8,128)(2,1)S(1)} %copy.15, f32[1024,1,1,16]{0,3,2,1:T(8,128)S(1)} %get-tuple-element.10, f32[1024,1,1,16]{0,3,2,1:T(8,128)S(1)} %get-tuple-element.9), kind=kOutput, calls=%fused_computation.4 | convolution fusion | flops 134545408 | bytes 8781824 | tf_op jit(solution)/shard_map/dot_general | solution.py:42
  383.2 0.0 copy-done.1
  383.2 0.0 copy-done.2
  383.2 0.0 all-gather.5.cloned.1.call-update
  383.3 83.6 %all-gather.5.cloned.1.call-done = bf16[4096,256]{0,1:T(8,128)(2,1)} async-done(((bf16[4096,16]{0,1:T(8,128)(2,1)}), bf16[4096,256]{0,1:T(8,128)(2,1)}) %all-gather.5.cloned.1.call-update) | async-done | bytes 2097168 | tf_op jit(solution)/shard_map/all_gather | solution.py:50
  466.8 4.1 copy.14
Async XLA Ops:
  7.2 165.7 %copy-start = (bf16[4096,256]{1,0:T(8,128)(2,1)S(1)}, bf16[4096,256]{1,0:T(8,128)(2,1)}, u32[]{:S(2)}) copy-start(bf16[4096,256]{1,0:T(8,128)(2,1)} %param.9) | copy-start | bytes 6291460
  7.2 60.2 %all-gather.3.cloned.1.call-start = ((), (), s32[]{:S(2)}) async-start(), calls=%async_computation.2 | async-start | bytes 8912896 | tf_op jit(solution)/shard_map/all_gather | solution.py:43
  7.9 164.9 %reduce-scatter.3.cloned.1.call-start = ((), (), s32[]{:S(2)}) async-start(), calls=%async_computation.3 | async-start | bytes 8912896 | tf_op jit(solution)/shard_map/reduce_scatter | solution.py:32
  95.3 280.7 %copy-start.3 = (f32[1024,1,1,16]{0,3,2,1:T(8,128)S(1)}, f32[1024,1,1,16]{0,3,2,1:T(8,128)}, u32[]{:S(2)}) copy-start(f32[1024,1,1,16]{0,3,2,1:T(8,128)} %param.11) | copy-start | bytes 196612
  95.3 280.7 %copy-start.4 = (f32[1024,1,1,16]{0,3,2,1:T(8,128)S(1)}, f32[1024,1,1,16]{0,3,2,1:T(8,128)}, u32[]{:S(2)}) copy-start(f32[1024,1,1,16]{0,3,2,1:T(8,128)} %param.10) | copy-start | bytes 196612
  95.4 280.7 %reduce-scatter.5.cloned.1.call-start = ((), (), s32[]{:S(2)}) async-start(), calls=%async_computation.4 | async-start | bytes 557056 | tf_op jit(solution)/shard_map/reduce_scatter | solution.py:35
  172.8 294.0 %all-gather.5.cloned.1.call-start = ((), (), s32[]{:S(2)}) async-start(), calls=%async_computation.5 | async-start | bytes 2228224 | tf_op jit(solution)/shard_map/all_gather | solution.py:50
  376.8 6.4 %copy-start.1 = (f32[1024,1,1,16]{0,3,2,1:T(8,128)}, f32[1024,1,1,16]{0,3,2,1:T(8,128)S(1)}, u32[]{:S(2)}) copy-start(f32[1024,1,1,16]{0,3,2,1:T(8,128)S(1)} %get-tuple-element.9) | copy-start | bytes 196612
  376.8 6.4 %copy-start.2 = (f32[1024,1,1,16]{0,3,2,1:T(8,128)}, f32[1024,1,1,16]{0,3,2,1:T(8,128)S(1)}, u32[]{:S(2)}) copy-start(f32[1024,1,1,16]{0,3,2,1:T(8,128)S(1)} %get-tuple-element.10) | copy-start | bytes 196612
Sparse Core Ops, SparseCore 0:
  9.9 57.5 all-gather.2
  95.5 77.2 reduce-scatter.2
  176.6 199.3 reduce-scatter.4
  383.4 83.4 all-gather.4
where the time goes:
time: 479 us; the launch traced here: 477 us
  waiting for transfers between devices  424 us (89%)
  matrix products  22.3 us (5%)
  local copies, waits for them, and re-layouts  16.7 us (3%)
  between operations  13.8 us (3%)
    reduce_scatter x1, waiting for transfers between devices, body(): lax.psum_scatter(partial_sum, 'dp', scatter_dimension=2, tiled=True)  202 us
    all_gather x1, waiting for transfers between devices, body(): new_weight = lax.all_gather(fresh, 'dp', axis=1, tiled=True)  83.6 us
    reduce_scatter x1, waiting for transfers between devices, body(): lax.psum_scatter(grouped.astype(jnp.bfloat16), 'fsdp', scatter_dimension=...  77.4 us
    all_gather x1, waiting for transfers between devices, body(): lax.all_gather(basis, 'fsdp', axis=0, tiled=True)  59.5 us
    dot_general x1, matrix products, body(): lax.dot_general(projected, cotangent, (((0,), (0,)), ((), ())), preferred...  16 us
    convert_element_type x1, local copies, waits for them, and re-layouts, body(): grouped.astype(jnp.bfloat16)  11.9 us
  transfers between devices with their start and end apart: 4, of which 4 were waited for; matrix products, arithmetic and copies ran while one was open for 0% of the time, Pallas kernels for 0%

commit v1 on v0

v1 whole, which is shorter than its diff:
```python
import math

import jax
import jax.numpy as jnp
from jax import lax
from jax.sharding import PartitionSpec as P

beta_one = 0.9
beta_two = 0.999
corr_one = 1.0 - math.exp(1000.0 * math.log(0.9))
corr_two = 1.0 - math.exp(1000.0 * math.log(0.999))
epsilon = 1e-08
rate = 0.5


def body(activations, cotangent, basis, weight, first, second):
    low_rank = basis.shape[1]
    owned = first.shape[-1]
    rows = lax.all_gather(basis, "fsdp", axis=0, tiled=True)
    projected = jnp.dot(activations, rows, preferred_element_type=jnp.float32)
    projected = projected.astype(jnp.bfloat16)
    gradient = lax.dot_general(
        cotangent, projected, (((0,), (0,)), ((), ())), preferred_element_type=jnp.float32
    )
    partial_sum = lax.psum_scatter(
        gradient.astype(jnp.bfloat16), "fsdp", scatter_dimension=0, tiled=True
    )
    summed = lax.psum_scatter(partial_sum, "dp", scatter_dimension=0, tiled=True)
    summed = summed.astype(jnp.float32)
    moment_one = beta_one * first.reshape(low_rank, owned).T + (1.0 - beta_one) * summed
    moment_two = beta_two * second.reshape(low_rank, owned).T + (1.0 - beta_two) * summed * summed
    update = moment_one / corr_one / (jnp.sqrt(moment_two / corr_two) + epsilon)
    update = lax.all_gather(update.astype(jnp.bfloat16), "dp", axis=0, tiled=True)
    expanded = lax.dot_general(
        rows, update, (((1,), (1,)), ((), ())), preferred_element_type=jnp.float32
    )
    new_weight = (weight.astype(jnp.float32) - rate * expanded).astype(jnp.bfloat16)
    return (new_weight, moment_one.T.reshape(first.shape), moment_two.T.reshape(first.shape))


def solution(mesh):
    in_specs = (
        P(("dp", "fsdp"), None),
        P(("dp", "fsdp"), None),
        P("fsdp", None),
        P(None, "fsdp"),
        P(None, "fsdp", "dp", None),
        P(None, "fsdp", "dp", None),
    )
    out_specs = (P(None, "fsdp"), P(None, "fsdp", "dp", None), P(None, "fsdp", "dp", None))
    return jax.shard_map(body, mesh=mesh, in_specs=in_specs, out_specs=out_specs, check_vma=False)
```

time: 479 us -> 423 us (0.88)
  waiting for transfers between devices: 424 us -> 336 us
  blocking collectives: 0 us -> 41.1 us
  local copies, waits for them, and re-layouts: 16.7 us -> 7.42 us
    all_gather x2 -> x1, waiting for transfers between devices: 143 us -> 59.5 us  [body(): rows = lax.all_gather(basis, 'fsdp', axis=0, tiled=True)]
    all_gather x0 -> x1, blocking collectives: none -> 41.1 us  [body(): lax.all_gather(update.astype(jnp.bfloat16), 'dp', axis=0, tiled=True)]
    convert_element_type x1 -> x0, local copies, waits for them, and re-layouts: 11.9 us -> none  [body(): grouped.astype(jnp.bfloat16)]
  transfers between devices with their start and end apart: 4 -> 3, of which waited for: 4 -> 3; matrix products, arithmetic and copies ran while one was open for 0% -> 1% of each run, Pallas kernels for 0% -> 0%
where the time goes in v1:
time: 423 us; the launch traced here: 422 us
  waiting for transfers between devices  336 us (79%)
  blocking collectives  41.1 us (10%)
  matrix products  22.3 us (5%)
  between operations  13.8 us (3%)
  local copies, waits for them, and re-layouts  7.42 us (2%)
    reduce_scatter x1, waiting for transfers between devices, body(): lax.psum_scatter(partial_sum, 'dp', scatter_dimension=0, tiled=True)  199 us
    reduce_scatter x1, waiting for transfers between devices, body(): lax.psum_scatter(gradient.astype(jnp.bfloat16), 'fsdp', scatter_dimension...  77.1 us
    all_gather x1, waiting for transfers between devices, body(): rows = lax.all_gather(basis, 'fsdp', axis=0, tiled=True)  59.5 us
    all_gather x1, blocking collectives, body(): lax.all_gather(update.astype(jnp.bfloat16), 'dp', axis=0, tiled=True)  41.1 us
    dot_general x1, matrix products, body(): lax.dot_general(cotangent, projected, (((0,), (0,)), ((), ())), preferred...  16 us
  transfers between devices with their start and end apart: 3, of which 3 were waited for; matrix products, arithmetic and copies ran while one was open for 1% of the time, Pallas kernels for 0%

profile of v1, /device:TPU:8, one launch (start us, length us, event | category | flops | bytes accessed | tf_op | source)
XLA Modules:
  0.0 422.2 jit_solution(4110558480536674385)
XLA Ops:
  7.2 0.0 all-gather.2.cloned.1.call-start
  7.2 0.7 all-gather.2.cloned.1.call-update
  7.9 0.0 reduce-scatter.5.cloned.1.call-start
  7.9 59.5 %all-gather.2.cloned.1.call-done = bf16[4096,1024]{1,0:T(8,128)(2,1)} async-done(((bf16[256,1024]{1,0:T(8,128)(2,1)}), bf16[4096,1024]{1,0:T(8,128)(2,1)}) %all-gather.2.cloned.1.call-update) | async-done | bytes 8388624 | tf_op jit(solution)/shard_map/all_gather | solution.py:19
  67.4 16.0 %convert_bitcast_fusion = bf16[4096,1024]{0,1:T(8,128)(2,1)} fusion(bf16[512,4096]{1,0:T(8,128)(2,1)} %param.7, bf16[512,4096]{1,0:T(8,128)(2,1)} %param.6, bf16[4096,1024]{1,0:T(8,128)(2,1)} %all-gather.2.cloned.1.call-done), kind=kOutput, calls=%fused_computation | convolution fusion | flops 8594653184 | bytes 25165824 | tf_op jit(solution)/shard_map/dot_general | solution.py:22
  83.4 0.0 copy-start
  83.4 0.0 reduce-scatter.5.cloned.1.call-update
  83.4 0.0 copy-start.1
  83.4 0.0 copy-start.2
  83.5 0.0 reduce-scatter.7.cloned.1.call-start
  83.5 77.1 %reduce-scatter.5.cloned.1.call-done = bf16[256,1024]{0,1:T(8,128)(2,1)} async-done(((bf16[4096,1024]{0,1:T(8,128)(2,1)}), bf16[256,1024]{0,1:T(8,128)(2,1)}) %reduce-scatter.5.cloned.1.call-update) | async-done | bytes 524304 | tf_op jit(solution)/shard_map/reduce_scatter | solution.py:25
  160.6 2.1 copy.25
  162.6 0.0 reduce-scatter.7.cloned.1.call-update
  162.7 0.0 copy-done
  162.7 2.9 copy.22
  165.5 198.8 %reduce-scatter.7.cloned.1.call-done = bf16[16,1024]{1,0:T(8,128)(2,1)} async-done(((bf16[256,1024]{1,0:T(8,128)(2,1)}), bf16[16,1024]{1,0:T(8,128)(2,1)}) %reduce-scatter.7.cloned.1.call-update) | async-done | bytes 32784 | tf_op jit(solution)/shard_map/reduce_scatter | solution.py:28
  364.3 0.0 copy-done.1
  364.3 0.0 copy-done.2
  364.3 1.4 fusion.6
  365.8 41.1 %all_gather.7 = bf16[256,1024]{1,0:T(8,128)(2,1)S(1)} all-gather(bf16[16,1024]{1,0:T(8,128)(2,1)S(1)} %get-tuple-element.13), channel_id=1, replica_groups=mesh['dp'=16,'fsdp'=16] {'dp'}, dimensions={0}, use_global_device_ids=true | all-gather | bytes 557056 | tf_op jit(solution)/shard_map/all_gather | solution.py:33
  406.9 6.3 %fusion.2 = bf16[4096,256]{0,1:T(8,128)(2,1)S(1)} fusion(bf16[256,1024]{1,0:T(8,128)(2,1)S(1)} %all_gather.7, bf16[4096,1024]{1,0:T(8,128)(2,1)} %all-gather.2.cloned.1.call-done, bf16[4096,256]{0,1:T(8,128)(2,1)} %copy.22), kind=kOutput, calls=%fused_computation.4 | convolution fusion | flops 2151677952 | bytes 13107200 | tf_op jit(solution)/shard_map/dot_general | solution.py:34
  413.2 2.5 copy.24
Async XLA Ops:
  7.2 60.2 %all-gather.2.cloned.1.call-start = ((), (), s32[]{:S(2)}) async-start(), calls=%async_computation.2 | async-start | bytes 8912896 | tf_op jit(solution)/shard_map/all_gather | solution.py:19
  7.9 152.7 %reduce-scatter.5.cloned.1.call-start = ((), (), s32[]{:S(2)}) async-start(), calls=%async_computation.3 | async-start | bytes 8912896 | tf_op jit(solution)/shard_map/reduce_scatter | solution.py:25
  83.4 79.3 %copy-start = (bf16[4096,256]{1,0:T(8,128)(2,1)S(1)}, bf16[4096,256]{1,0:T(8,128)(2,1)}, u32[]{:S(2)}) copy-start(bf16[4096,256]{1,0:T(8,128)(2,1)} %param.9) | copy-start | bytes 6291460
  83.4 280.9 %copy-start.1 = (f32[1024,1,1,16]{0,3,2,1:T(8,128)S(1)}, f32[1024,1,1,16]{0,3,2,1:T(8,128)}, u32[]{:S(2)}) copy-start(f32[1024,1,1,16]{0,3,2,1:T(8,128)} %param.11) | copy-start | bytes 196612
  83.4 280.9 %copy-start.2 = (f32[1024,1,1,16]{0,3,2,1:T(8,128)S(1)}, f32[1024,1,1,16]{0,3,2,1:T(8,128)}, u32[]{:S(2)}) copy-start(f32[1024,1,1,16]{0,3,2,1:T(8,128)} %param.10) | copy-start | bytes 196612
  83.5 280.9 %reduce-scatter.7.cloned.1.call-start = ((), (), s32[]{:S(2)}) async-start(), calls=%async_computation.4 | async-start | bytes 557056 | tf_op jit(solution)/shard_map/reduce_scatter | solution.py:28
Sparse Core Ops, SparseCore 0:
  9.9 57.5 all-gather.1
  83.5 76.9 reduce-scatter.4
  164.4 199.8 reduce-scatter.6

commit v2 on v1

v2 whole, which is shorter than its diff:
```python
import math

import jax
import jax.numpy as jnp
from jax import lax
from jax.experimental import pallas as pl
from jax.experimental.pallas import tpu as pltpu
from jax.sharding import PartitionSpec as P

beta_one = 0.9
beta_two = 0.999
corr_one = 1.0 - math.exp(1000.0 * math.log(0.9))
corr_two = 1.0 - math.exp(1000.0 * math.log(0.999))
epsilon = 1e-08
rate = 0.5

AXES = ("dp", "fsdp")
NX, NY, NZ = 4, 4, 8
RING_Y = (0, 2, 1, 3)
VMEM = 56 * 2**20


def place(x, y, z, c):
    return (z * 2 + y // 2) * 16 + ((y % 2) * 4 + x) * 2 + c


CHIPS = [(x, y, z) for z in range(NZ) for y in range(NY) for x in range(NX)]


def shift(value, dx=0, dy=0, swap=False):
    pairs = [
        (place(x, y, z, c), place((x + dx) % NX, (y + dy) % NY, z, 1 - c if swap else c))
        for x, y, z in CHIPS
        for c in range(2)
    ]
    return lax.ppermute(value, AXES, sorted(pairs))


def along_x(c):
    return [[place(x, y, z, c) for x in range(NX)] for z in range(NZ) for y in range(NY)]


def along_y(c):
    return [[place(x, y, z, c) for y in RING_Y] for z in range(NZ) for x in range(NX)]


def along_zc():
    return [
        [place(x, y, z, c) for z in range(NZ) for c in range(2)]
        for y in range(NY)
        for x in range(NX)
    ]


def exchange(value, groups):
    return lax.all_to_all(value, AXES, 0, 0, tiled=True, axis_index_groups=groups)


def dot(a, b, dims):
    return lax.dot_general(a, b, (dims, ((), ())), preferred_element_type=jnp.float32)


def project_kernel(layout, first, order, own, other, *refs):
    count = sum(layout)
    pieces, rest = refs[:count], refs[count:]
    if first:
        total, stacked = rest
        result = None
    else:
        before, result, stacked, total = rest
    step = pl.program_id(0)
    half = own.shape[0]

    @pl.when(step == 0)
    def _():
        total[...] = jnp.zeros_like(total) if first else before[...]

    at = 0
    for j, n in enumerate(layout):
        mine = pieces[at : at + n]
        at += n

        @pl.when(step == j)
        def _(mine=mine):
            done = 0
            for piece in mine:
                rows = piece.shape[0]
                stacked[0, done : done + rows, :] = piece[...]
                for i, block in enumerate((own, other)):
                    total[i * half : (i + 1) * half, :] += dot(
                        block[:, done : done + rows], piece[...], ((1,), (0,))
                    )
                done += rows

    if not first:

        @pl.when(step == len(layout) - 1)
        def _():
            result[...] = total[...].astype(result.dtype)


def project(order, own, other, groups, before=None):
    layout = [len(g) for g in groups]
    pieces = [p for g in groups for p in g]
    n, (half, _) = len(groups), own.shape
    depth, low = sum(p.shape[0] for p in groups[0]), pieces[0].shape[1]
    whole = lambda a: pl.BlockSpec(a.shape, lambda j, o: (0,) * a.ndim)
    block = pl.BlockSpec((half, depth), lambda j, o: (0, o[j]))
    stacked = jax.ShapeDtypeStruct((n, depth, low), jnp.bfloat16)
    stack_spec = pl.BlockSpec((1, depth, low), lambda j, o: (j, 0, 0))
    total = jax.ShapeDtypeStruct((2 * half, low), jnp.float32)
    ins = [block, block] + [whole(p) for p in pieces]
    args = [own, other] + pieces
    scratch = []
    if before is None:
        outs, out_specs = [total, stacked], [whole(total), stack_spec]
    else:
        ins.append(whole(before))
        args.append(before)
        result = jax.ShapeDtypeStruct(total.shape, jnp.bfloat16)
        outs, out_specs = [result, stacked], [whole(result), stack_spec]
        scratch = [pltpu.VMEM(total.shape, jnp.float32)]

    def kernel(*refs):
        project_kernel(layout, before is None, *refs)

    return pl.pallas_call(
        kernel,
        grid_spec=pltpu.PrefetchScalarGridSpec(
            num_scalar_prefetch=1,
            grid=(n,),
            in_specs=ins,
            out_specs=out_specs,
            scratch_shapes=scratch,
        ),
        out_shape=outs,
        cost_estimate=pl.CostEstimate(
            flops=4 * half * depth * n * low, bytes_accessed=16 * 2**20, transcendentals=0
        ),
        compiler_params=pltpu.CompilerParams(vmem_limit_bytes=VMEM),
    )(order, *args)


def gradient_kernel(core, own, other, projected, out, tile):
    half = own.shape[0]
    high = pl.program_id(1)

    @pl.when(high == 0)
    def _():
        total = dot(own[...], projected[:half, :], ((0,), (0,)))
        total += dot(other[...], projected[half:, :], ((0,), (0,)))
        tile[...] = total.astype(tile.dtype)

    for h in range(2):

        @pl.when(high == h)
        def _(h=h):
            for z in range(NZ):
                for c in range(2):
                    at = c * 256 + z * 32 + h * 16
                    to = z * 32 + c * 16
                    out[0, 0, to : to + 16, :] = tile[at : at + 16, :]


def gradient(core, own, other, projected):
    half, width = own.shape
    low = projected.shape[1]
    cols = width // 8

    def place_out(t, h, c):
        x, y = t % 4, (t // 4) * 2 + h
        return jnp.where(c[0] == 0, x, y), jnp.where(c[0] == 0, y, x), 0, 0

    block = pl.BlockSpec((half, cols), lambda t, h, c: (0, t))
    return pl.pallas_call(
        gradient_kernel,
        grid_spec=pltpu.PrefetchScalarGridSpec(
            num_scalar_prefetch=1,
            grid=(8, 2),
            in_specs=[
                block,
                block,
                pl.BlockSpec(projected.shape, lambda t, h, c: (0, 0)),
            ],
            out_specs=pl.BlockSpec((1, 1, cols // 2, low), place_out),
            scratch_shapes=[pltpu.VMEM((cols, low), jnp.bfloat16)],
        ),
        out_shape=jax.ShapeDtypeStruct((4, 4, cols // 2, low), jnp.bfloat16),
        cost_estimate=pl.CostEstimate(
            flops=4 * half * width * low, bytes_accessed=14 * 2**20, transcendentals=0
        ),
        compiler_params=pltpu.CompilerParams(vmem_limit_bytes=VMEM),
    )(core, own, other, projected)


def expand_kernel(order, core, mine_a, mine_b, rest_a, rest_b, near, far, weight, out):
    step = pl.program_id(0)

    def write(mine, rest):
        total = dot(mine[0], near[...], ((1,), (1,)))
        total += dot(rest[0], far[...], ((1,), (1,)))
        out[...] = (weight[...].astype(jnp.float32) - rate * total).astype(out.dtype)

    @pl.when(step < 4)
    def _():
        write(mine_a, rest_a)

    @pl.when(step >= 4)
    def _():
        write(mine_b, rest_b)


def expand(order, core, mine, rest, update, weight):
    _, depth, low = mine[0].shape
    cols = weight.shape[1]
    early = pl.BlockSpec((1, depth, low), lambda j, o, c: (jnp.minimum(j, 3), 0, 0))
    late = pl.BlockSpec((1, depth, low), lambda j, o, c: (jnp.maximum(j - 4, 0), 0, 0))
    rows = pl.BlockSpec((depth, cols), lambda j, o, c: (o[j], 0))
    return pl.pallas_call(
        expand_kernel,
        grid_spec=pltpu.PrefetchScalarGridSpec(
            num_scalar_prefetch=2,
            grid=(8,),
            in_specs=[
                early,
                late,
                early,
                late,
                pl.BlockSpec((cols, low), lambda j, o, c: (0, c[0])),
                pl.BlockSpec((cols, low), lambda j, o, c: (0, 1 - c[0])),
                rows,
            ],
            out_specs=rows,
        ),
        out_shape=jax.ShapeDtypeStruct(weight.shape, weight.dtype),
        cost_estimate=pl.CostEstimate(
            flops=4 * weight.size * low, bytes_accessed=13 * 2**20, transcendentals=0
        ),
        compiler_params=pltpu.CompilerParams(vmem_limit_bytes=VMEM),
    )(order, core, *mine, *rest, update, update, weight)


def added(value):
    return jnp.sum(value.astype(jnp.float32), axis=0).astype(jnp.bfloat16)


def body(activations, cotangent, basis, weight, first, second):
    low_rank = basis.shape[1]
    half = low_rank // 2
    owned = first.shape[-1]
    f = lax.axis_index("fsdp")
    core, x, y_lo = f % 2, (f // 2) % 4, f // 8
    order = jnp.stack(
        [
            side * 4 + (x + step) % 4
            for side, step in (
                (y_lo, 0),
                (y_lo, 3),
                (y_lo, 1),
                (1 - y_lo, 0),
                (y_lo, 2),
                (1 - y_lo, 3),
                (1 - y_lo, 1),
                (1 - y_lo, 2),
            )
        ]
    ).astype(jnp.int32)
    core_id = core.reshape(1).astype(jnp.int32)

    left, right = basis[:, :half], basis[:, half:]
    kept = jnp.where(core == 0, left, right)
    came = shift(jnp.where(core == 0, right, left), swap=True)
    top = jnp.where(core == 0, kept, came)
    bottom = jnp.where(core == 0, came, kept)
    chip = jnp.concatenate([top, bottom], axis=0)
    other_activations = shift(activations, swap=True)
    other_cotangent = shift(cotangent, swap=True)

    back = shift(chip, dx=1)
    ahead = shift(chip, dx=-1)
    across_top = shift(top, dy=1)
    across_bottom = shift(bottom, dy=-1)
    rows = top.shape[0]
    far_top = shift(back[:rows], dx=1)
    far_bottom = shift(ahead[rows:], dx=-1)
    across_back = shift(back, dy=1)
    across_ahead = shift(ahead, dy=-1)
    across_far_top = shift(far_top, dy=1)
    across_far_bottom = shift(far_bottom, dy=-1)

    begun, stacked_a = project(
        order[:4],
        activations,
        other_activations,
        [(chip,), (back,), (ahead,), (across_top, across_bottom)],
    )
    projected, stacked_b = project(
        order[4:],
        activations,
        other_activations,
        [
            (far_top, far_bottom),
            (across_back,),
            (across_ahead,),
            (across_far_top, across_far_bottom),
        ],
        begun,
    )
    rest = (shift(stacked_a, swap=True), shift(stacked_b, swap=True))

    terms = gradient(core_id, cotangent, other_cotangent, projected)
    terms = added(exchange(terms, along_x(0) + along_y(1)))
    terms = added(exchange(terms, along_y(0) + along_x(1)))
    terms = exchange(terms.reshape(16, owned, half), along_zc())
    summed = jnp.sum(terms.reshape(NZ, 2, owned, half).astype(jnp.float32), axis=0)
    summed = summed.transpose(1, 0, 2).reshape(owned, low_rank)

    moment_one = beta_one * first.reshape(low_rank, owned).T + (1.0 - beta_one) * summed
    moment_two = beta_two * second.reshape(low_rank, owned).T + (1.0 - beta_two) * summed * summed
    update = moment_one / corr_one / (jnp.sqrt(moment_two / corr_two) + epsilon)
    update = update.astype(jnp.bfloat16)
    copies = jnp.broadcast_to(update[None], (16, owned, low_rank))
    update = lax.all_to_all(copies, "dp", 0, 0, tiled=True).reshape(16 * owned, low_rank)

    new_weight = expand(order, core_id, (stacked_a, stacked_b), rest, update, weight)
    return (new_weight, moment_one.T.reshape(first.shape), moment_two.T.reshape(first.shape))


def solution(mesh):
    in_specs = (
        P(("dp", "fsdp"), None),
        P(("dp", "fsdp"), None),
        P("fsdp", None),
        P(None, "fsdp"),
        P(None, "fsdp", "dp", None),
        P(None, "fsdp", "dp", None),
    )
    out_specs = (P(None, "fsdp"), P(None, "fsdp", "dp", None), P(None, "fsdp", "dp", None))
    return jax.shard_map(body, mesh=mesh, in_specs=in_specs, out_specs=out_specs, check_vma=False)
```

time: 423 us -> 190 us (0.45)
  waiting for transfers between devices: 336 us -> 52.9 us
  Pallas kernels: 0 us -> 44.2 us
  starting transfers between devices: 0.12 us -> 26 us
  matrix products: 22.3 us -> 0 us
  between operations: 13.8 us -> 0.8 us
  blocking collectives: 41.1 us -> 52.9 us
  other arithmetic: 1.45 us -> 8.46 us
    reduce_scatter x2 -> x0, waiting for transfers between devices: 276 us -> none  [the longest x1 199 us: body(): lax.psum_scatter(partial_sum, 'dp', scatter_dimension=0, tiled=True)]
    all_gather x1 -> x0, waiting for transfers between devices: 59.5 us -> none  [body(): rows = lax.all_gather(basis, 'fsdp', axis=0, tiled=True)]
    all_to_all x0 -> x2, blocking collectives: none -> 52.9 us  [exchange(): lax.all_to_all(value, AXES, 0, 0, tiled=True, axis_index_groups=groups)]
    pallas_call x0 -> x4, Pallas kernels: none -> 44.2 us  [the longest x1 18.3 us: gradient(): pl.pallas_call(gradient_kernel, grid_spec=pltpu.PrefetchScalarGridSpec(nu...]
    all_gather x1 -> x0, blocking collectives: 41.1 us -> none  [body(): lax.all_gather(update.astype(jnp.bfloat16), 'dp', axis=0, tiled=True)]
    all_to_all x0 -> x2, waiting for transfers between devices: none -> 27.6 us  [the longest x1 19.3 us: body(): lax.all_to_all(copies, 'dp', 0, 0, tiled=True).reshape(16 * owned, low_rank)]
    ppermute x0 -> x15, waiting for transfers between devices: none -> 25.3 us  [shift(): return lax.ppermute(value, AXES, sorted(pairs))]
    dot_general x2 -> x0, matrix products: 22.3 us -> none  [the longest x1 16 us: body(): lax.dot_general(cotangent, projected, (((0,), (0,)), ((), ())), preferred...]
  transfers between devices with their start and end apart: 3 -> 17, of which waited for: 3 -> 8; matrix products, arithmetic and copies ran while one was open for 1% -> 3% of each run, Pallas kernels for 0% -> 8%
where the time goes in v2:
time: 190 us; the launch traced here: 189 us
  waiting for transfers between devices  52.9 us (28%)
  blocking collectives  52.9 us (28%)
  Pallas kernels  44.2 us (23%)
  starting transfers between devices  26 us (14%)
  other arithmetic  8.46 us (4%)
  local copies, waits for them, and re-layouts  3.45 us (2%)
    all_to_all x2, blocking collectives, exchange(): lax.all_to_all(value, AXES, 0, 0, tiled=True, axis_index_groups=groups)  52.9 us
    ppermute x15, waiting for transfers between devices, shift(): return lax.ppermute(value, AXES, sorted(pairs))  25.3 us
    all_to_all x1, waiting for transfers between devices, body(): lax.all_to_all(copies, 'dp', 0, 0, tiled=True).reshape(16 * owned, low_rank)  19.3 us
    pallas_call x1, Pallas kernels, gradient(): pl.pallas_call(gradient_kernel, grid_spec=pltpu.PrefetchScalarGridSpec(nu...  18.3 us
    ppermute x15, starting transfers between devices, shift(): return lax.ppermute(value, AXES, sorted(pairs))  16.6 us
    pallas_call x2, Pallas kernels, project(): pl.pallas_call(kernel, grid_spec=pltpu.PrefetchScalarGridSpec(num_scalar_...  15.9 us
    pallas_call x1, Pallas kernels, expand(): pl.pallas_call(expand_kernel, grid_spec=pltpu.PrefetchScalarGridSpec(num_...  10 us
    all_to_all x1, waiting for transfers between devices, exchange(): lax.all_to_all(value, AXES, 0, 0, tiled=True, axis_index_groups=groups)  8.31 us
  transfers between devices with their start and end apart: 17, of which 8 were waited for; matrix products, arithmetic and copies ran while one was open for 3% of the time, Pallas kernels for 8%

profile of v2, /device:TPU:8, one launch (start us, length us, event | category | flops | bytes accessed | tf_op | source)
XLA Modules:
  0.0 188.7 jit_solution(16235615563200826585)
XLA Ops:
  0.6 0.1 collective-permute-start
  0.7 0.5 collective-permute-start.14
  1.2 1.1 broadcast_select_fusion.2
  2.3 0.2 collective-permute-start.1
  2.5 6.1 %collective-permute-done.1 = bf16[256,512]{1,0:T(8,128)(2,1)S(1)} collective-permute-done((bf16[256,512]{1,0:T(8,128)(2,1)S(1)}, bf16[256,512]{1,0:T(8,128)(2,1)S(1)}, u32[]{:S(2)}, u32[]{:S(2)}) %collective-permute-start.1) | collective-permute-done | bytes 262176 | tf_op jit(solution)/shard_map/ppermute | solution.py:36
  8.6 1.1 broadcast_select_fusion.1
  9.8 1.6 collective-permute-start.2
  11.3 1.7 collective-permute-start.3
  13.1 1.6 collective-permute-start.4
  14.7 10.4 %collective-permute-done.2.refs_4_ = bf16[512,512]{1,0:T(8,128)(2,1)S(1)} collective-permute-done((bf16[512,512]{1,0:T(8,128)(2,1)S(1)}, bf16[512,512]{1,0:T(8,128)(2,1)S(1)}, u32[]{:S(2)}, u32[]{:S(2)}) %collective-permute-start.2) | collective-permute-done | bytes 524320 | tf_op jit(solution)/shard_map/ppermute | solution.py:36
  25.0 2.2 %collective-permute-start.5 = (bf16[256,512]{1,0:T(8,128)(2,1)S(1)}, bf16[256,512]{1,0:T(8,128)(2,1)}, u32[]{:S(2)}, u32[]{:S(2)}) collective-permute-start(bf16[256,512]{1,0:T(8,128)(2,1)S(1)} %get-tuple-element.12), channel_id=1, source_target_pairs={{0,24},{1,25},{2,26},{3,27},{4,28},{5,29},{6,30},{7,31},{8,0},{9,1... | collective-permute-start | bytes 786440 | tf_op jit(solution)/shard_map/ppermute | solution.py:36
  27.2 0.0 collective-permute-done.3.refs_5_
  27.3 0.1 collective-permute-start.6
  27.4 3.3 %collective-permute-start.7 = (bf16[256,512]{1,0:T(8,128)(2,1)S(1)}, bf16[256,512]{1,0:T(8,128)(2,1)S(1)}, u32[]{:S(2)}, u32[]{:S(2)}) collective-permute-start(bf16[256,512]{1,0:T(8,128)(2,1)S(1)} %slice.21), channel_id=1, source_target_pairs={{0,6},{1,7},{2,0},{3,1},{4,2},{5,3},{6,4},{7,5},{8,14},{9,15},{10,... | collective-permute-start | bytes 786440 | tf_op jit(solution)/shard_map/ppermute | solution.py:36
  30.7 2.0 %collective-permute-done.5.refs_7_ = bf16[256,512]{1,0:T(8,128)(2,1)} collective-permute-done((bf16[256,512]{1,0:T(8,128)(2,1)S(1)}, bf16[256,512]{1,0:T(8,128)(2,1)}, u32[]{:S(2)}, u32[]{:S(2)}) %collective-permute-start.5) | collective-permute-done | bytes 262176 | tf_op jit(solution)/shard_map/ppermute | solution.py:36
  32.7 1.6 collective-permute-start.8
  34.2 1.6 collective-permute-done.6.refs_3_
  35.8 1.3 collective-permute-start.9
  37.1 0.6 pad_add_fusion.refs_0_
  37.7 0.0 collective-permute-done.7.refs_4_
  37.7 0.7 collective-permute-start.10
  38.4 0.0 collective-permute-done.refs_2_
  38.4 1.3 collective-permute-start.11
  39.7 0.6 pad_add_fusion.1.refs_0_
  40.3 7.8 %shard_map.85 = (f32[1024,512]{1,0:T(8,128)}, bf16[4,512,512]{2,1,0:T(8,128)(2,1)}) custom-call(s32[4]{0:T(128)} %pad_add_fusion.refs_0_, bf16[512,4096]{1,0:T(8,128)(2,1)} %refs_1_.3, bf16[512,4096]{1,0:T(8,128)(2,1)} %collective-permute-done.refs_2_, bf16[512,512]{1,0:T(8,128)(2,1)} %copy-done.2, bf16[512,512]{1,0:T(8,128)(2,1)} %copy-done.3, ...), custom_call_target="tpu_custom_call" | custom-call | flops 2147483648 | bytes 16777216 | tf_op jit(solution)/shard_map/pallas_call | solution.py:127
  48.0 2.9 %collective-permute-done.10.refs_7_ = bf16[256,512]{1,0:T(8,128)(2,1)S(1)} collective-permute-done((bf16[256,512]{1,0:T(8,128)(2,1)S(1)}, bf16[256,512]{1,0:T(8,128)(2,1)S(1)}, u32[]{:S(2)}, u32[]{:S(2)}) %collective-permute-start.10) | collective-permute-done | bytes 262176 | tf_op jit(solution)/shard_map/ppermute | solution.py:36
  50.9 2.4 %collective-permute-done.11.refs_8_ = bf16[256,512]{1,0:T(8,128)(2,1)S(1)} collective-permute-done((bf16[256,512]{1,0:T(8,128)(2,1)S(1)}, bf16[256,512]{1,0:T(8,128)(2,1)S(1)}, u32[]{:S(2)}, u32[]{:S(2)}) %collective-permute-start.11) | collective-permute-done | bytes 262176 | tf_op jit(solution)/shard_map/ppermute | solution.py:36
  53.4 0.7 copy-done.10
  54.0 0.2 copy-done.5
  54.2 0.2 copy-done.6
  54.4 8.1 %shard_map.86 = (bf16[1024,512]{1,0:T(8,128)(2,1)}, bf16[4,512,512]{2,1,0:T(8,128)(2,1)}) custom-call(s32[4]{0:T(128)} %pad_add_fusion.1.refs_0_, bf16[512,4096]{1,0:T(8,128)(2,1)} %refs_1_.3, bf16[512,4096]{1,0:T(8,128)(2,1)} %collective-permute-done.refs_2_, bf16[256,512]{1,0:T(8,128)(2,1)} %copy-done.7, bf16[256,512]{1,0:T(8,128)(2,1)} %copy-done.8, ...), custom_call_target="tpu_custom_call" | custom-call | flops 2147483648 | bytes 16777216 | tf_op jit(solution)/shard_map/pallas_call | solution.py:127
  62.5 0.0 collective-permute-done.14.other
  62.5 18.3 %shard_map.87 = bf16[4,4,256,512]{3,2,1,0:T(8,128)(2,1)} custom-call(s32[1]{0:T(128)} %bitcast.8.core, bf16[512,4096]{1,0:T(8,128)(2,1)} %own.1, bf16[512,4096]{1,0:T(8,128)(2,1)} %collective-permute-done.14.other, bf16[1024,512]{1,0:T(8,128)(2,1)} %get-tuple-element.10.projected), custom_call_target="tpu_custom_call" | custom-call | flops 4294967296 | bytes 14680064 | tf_op jit(solution)/shard_map/pallas_call | solution.py:175
  80.8 33.4 %all_to_all.20 = bf16[4,4,256,512]{3,2,1,0:T(8,128)(2,1)} all-to-all(bf16[4,4,256,512]{3,2,1,0:T(8,128)(2,1)} %shard_map.87), channel_id=1, replica_groups={{0,2,4,6},{8,10,12,14},{16,18,20,22},{24,26,28,30},{32,34,36,38},{40,42..., dimensions={0} | all-to-all | bytes 8388608 | tf_op jit(solution)/shard_map/all_to_all | solution.py:56
  114.3 4.1 %reduce_sum.33 = bf16[4,256,512]{2,1,0:T(8,128)(2,1)} reduce(bf16[4,4,256,512]{3,2,1,0:T(8,128)(2,1)} %all_to_all.20, bf16[]{:T(256)} %constant.87.clone.1), dimensions={0}, to_apply=%region_0.1 | reduce | flops 1572864 | bytes 5242882 | tf_op jit(solution)/shard_map/reduce_sum | solution.py:244
  118.4 5.0 %all-to-all-start.1 = ((bf16[4,256,512]{2,1,0:T(8,128)(2,1)}), bf16[4,256,512]{2,1,0:T(8,128)(2,1)S(1)}, u32[]{:S(2)}, u32[]{:S(2)}) async-start(bf16[4,256,512]{2,1,0:T(8,128)(2,1)} %reduce_sum.33), calls=%async_computation.1 | async-start | bytes 2097152 | tf_op jit(solution)/shard_map/all_to_all | solution.py:56
  123.4 0.0 collective-permute-start.13
  123.4 0.5 collective-permute-start.12
  123.9 8.3 %all-to-all-done.1 = bf16[4,256,512]{2,1,0:T(8,128)(2,1)S(1)} async-done(((bf16[4,256,512]{2,1,0:T(8,128)(2,1)}), bf16[4,256,512]{2,1,0:T(8,128)(2,1)S(1)}, u32[]{:S(2)}, u32[]{:S(2)}) %all-to-all-start.1) | async-done | bytes 1048608 | tf_op jit(solution)/shard_map/all_to_all | solution.py:56
  132.2 0.2 reduce_sum.34
  132.4 19.5 %all_to_all.21 = bf16[16,16,512]{2,1,0:T(8,128)(2,1)S(1)} all-to-all(bf16[16,16,512]{2,1,0:T(8,128)(2,1)S(1)} %bitcast.42), channel_id=1, replica_groups={{0,1,32,33,64,65,96,97,128,129,160,161,192,193,224,225},{2,3,34,35,66,6..., dimensions={0} | all-to-all | bytes 524288 | tf_op jit(solution)/shard_map/all_to_all | solution.py:56
  152.0 0.7 fusion.2
  152.7 0.9 broadcast_in_dim.2
  153.6 4.4 %all-to-all-start.3 = ((bf16[16,16,1024]{2,1,0:T(8,128)(2,1)}), bf16[16,16,1024]{2,1,0:T(8,128)(2,1)S(1)}, u32[]{:S(2)}, u32[]{:S(2)}) async-start(bf16[16,16,1024]{2,1,0:T(8,128)(2,1)} %broadcast_in_dim.2), calls=%async_computation.3 | async-start | bytes 1048576 | tf_op jit(solution)/shard_map/all_to_all | solution.py:323
  157.9 0.7 stack.39.order
  158.6 19.3 %all-to-all-done.3 = bf16[16,16,1024]{2,1,0:T(8,128)(2,1)S(1)} async-done(((bf16[16,16,1024]{2,1,0:T(8,128)(2,1)}), bf16[16,16,1024]{2,1,0:T(8,128)(2,1)S(1)}, u32[]{:S(2)}, u32[]{:S(2)}) %all-to-all-start.3) | async-done | bytes 524320 | tf_op jit(solution)/shard_map/all_to_all | solution.py:323
  177.9 0.8 copy-done
  178.7 10.0 %shard_map.88 = bf16[4096,256]{1,0:T(8,128)(2,1)} custom-call(s32[8]{0:T(128)} %stack.39.order, s32[1]{0:T(128)} %bitcast.8.core, bf16[4,512,512]{2,1,0:T(8,128)(2,1)} %get-tuple-element.7.mine_a, bf16[4,512,512]{2,1,0:T(8,128)(2,1)} %get-tuple-element.9.mine_b, bf16[4,512,512]{2,1,0:T(8,128)(2,1)} %collective-permute-done.12.rest_a, ...), custom_call_target="tpu_custom_call" | custom-call | flops 2147483648 | bytes 13631488 | tf_op jit(solution)/shard_map/pallas_call | solution.py:219
  (34 shorter events, 0.2 us)
Async XLA Ops:
  0.6 37.8 %collective-permute-start = (bf16[512,4096]{1,0:T(8,128)(2,1)}, bf16[512,4096]{1,0:T(8,128)(2,1)}, u32[]{:S(2)}, u32[]{:S(2)}) collective-permute-start(bf16[512,4096]{1,0:T(8,128)(2,1)} %refs_1_.3), channel_id=1, source_target_pairs={{0,1},{1,0},{2,3},{3,2},{4,5},{5,4},{6,7},{7,6},{8,9},{9,8},{10,11... | collective-permute-start | bytes 12582920 | tf_op jit(solution)/shard_map/ppermute | solution.py:36
  0.7 61.8 %collective-permute-start.14 = (bf16[512,4096]{1,0:T(8,128)(2,1)}, bf16[512,4096]{1,0:T(8,128)(2,1)}, u32[]{:S(2)}, u32[]{:S(2)}) collective-permute-start(bf16[512,4096]{1,0:T(8,128)(2,1)} %own.1), channel_id=1, source_target_pairs={{0,1},{1,0},{2,3},{3,2},{4,5},{5,4},{6,7},{7,6},{8,9},{9,8},{10,11... | collective-permute-start | bytes 12582920 | tf_op jit(solution)/shard_map/ppermute | solution.py:36
  2.3 6.3 %collective-permute-start.1 = (bf16[256,512]{1,0:T(8,128)(2,1)S(1)}, bf16[256,512]{1,0:T(8,128)(2,1)S(1)}, u32[]{:S(2)}, u32[]{:S(2)}) collective-permute-start(bf16[256,512]{1,0:T(8,128)(2,1)S(1)} %broadcast_select_fusion.2), channel_id=1, source_target_pairs={{0,1},{1,0},{2,3},{3,2},{4,5},{5,4},{6,7},{7,6},{8,9},{9,8},{10,11... | collective-permute-start | bytes 786440 | tf_op jit(solution)/shard_map/ppermute | solution.py:36
  9.8 30.5 %copy-start.2 = (bf16[512,512]{1,0:T(8,128)(2,1)}, bf16[512,512]{1,0:T(8,128)(2,1)S(1)}, u32[]{:S(2)}) copy-start(bf16[512,512]{1,0:T(8,128)(2,1)S(1)} %pad_maximum_fusion.refs_3_) | copy-start | bytes 1572868
  9.8 15.3 %collective-permute-start.2 = (bf16[512,512]{1,0:T(8,128)(2,1)S(1)}, bf16[512,512]{1,0:T(8,128)(2,1)S(1)}, u32[]{:S(2)}, u32[]{:S(2)}) collective-permute-start(bf16[512,512]{1,0:T(8,128)(2,1)S(1)} %pad_maximum_fusion.refs_3_), channel_id=1, source_target_pairs={{0,2},{1,3},{2,4},{3,5},{4,6},{5,7},{6,0},{7,1},{8,10},{9,11},{10,... | collective-permute-start | bytes 1572872 | tf_op jit(solution)/shard_map/ppermute | solution.py:36
  11.3 15.9 %collective-permute-start.3 = (bf16[512,512]{1,0:T(8,128)(2,1)S(1)}, bf16[512,512]{1,0:T(8,128)(2,1)S(1)}, u32[]{:S(2)}, u32[]{:S(2)}) collective-permute-start(bf16[512,512]{1,0:T(8,128)(2,1)S(1)} %pad_maximum_fusion.refs_3_), channel_id=1, source_target_pairs={{0,6},{1,7},{2,0},{3,1},{4,2},{5,3},{6,4},{7,5},{8,14},{9,15},{10,... | collective-permute-start | bytes 1572872 | tf_op jit(solution)/shard_map/ppermute | solution.py:36
  13.1 14.3 %collective-permute-start.4 = (bf16[256,512]{1,0:T(8,128)(2,1)S(1)}, bf16[256,512]{1,0:T(8,128)(2,1)S(1)}, u32[]{:S(2)}, u32[]{:S(2)}) collective-permute-start(bf16[256,512]{1,0:T(8,128)(2,1)S(1)} %get-tuple-element.11), channel_id=1, source_target_pairs={{0,8},{1,9},{2,10},{3,11},{4,12},{5,13},{6,14},{7,15},{8,16},{9,17... | collective-permute-start | bytes 786440 | tf_op jit(solution)/shard_map/ppermute | solution.py:36
  25.0 15.3 %copy-start.3 = (bf16[512,512]{1,0:T(8,128)(2,1)}, bf16[512,512]{1,0:T(8,128)(2,1)S(1)}, u32[]{:S(2)}) copy-start(bf16[512,512]{1,0:T(8,128)(2,1)S(1)} %collective-permute-done.2.refs_4_) | copy-start | bytes 1572868
  25.0 7.6 %collective-permute-start.5 = (bf16[256,512]{1,0:T(8,128)(2,1)S(1)}, bf16[256,512]{1,0:T(8,128)(2,1)}, u32[]{:S(2)}, u32[]{:S(2)}) collective-permute-start(bf16[256,512]{1,0:T(8,128)(2,1)S(1)} %get-tuple-element.12), channel_id=1, source_target_pairs={{0,24},{1,25},{2,26},{3,27},{4,28},{5,29},{6,30},{7,31},{8,0},{9,1... | collective-permute-start | bytes 786440 | tf_op jit(solution)/shard_map/ppermute | solution.py:36
  27.2 13.0 %copy-start.4 = (bf16[512,512]{1,0:T(8,128)(2,1)}, bf16[512,512]{1,0:T(8,128)(2,1)S(1)}, u32[]{:S(2)}) copy-start(bf16[512,512]{1,0:T(8,128)(2,1)S(1)} %collective-permute-done.3.refs_5_) | copy-start | bytes 1572868
  27.3 8.5 %collective-permute-start.6 = (bf16[256,512]{1,0:T(8,128)(2,1)S(1)}, bf16[256,512]{1,0:T(8,128)(2,1)S(1)}, u32[]{:S(2)}, u32[]{:S(2)}) collective-permute-start(bf16[256,512]{1,0:T(8,128)(2,1)S(1)} %slice.20), channel_id=1, source_target_pairs={{0,2},{1,3},{2,4},{3,5},{4,6},{5,7},{6,0},{7,1},{8,10},{9,11},{10,... | collective-permute-start | bytes 786440 | tf_op jit(solution)/shard_map/ppermute | solution.py:36
  27.4 6.8 %copy-start.11 = (bf16[256,512]{1,0:T(8,128)(2,1)}, bf16[256,512]{1,0:T(8,128)(2,1)S(1)}, u32[]{:S(2)}) copy-start(bf16[256,512]{1,0:T(8,128)(2,1)S(1)} %collective-permute-done.4.refs_6_) | copy-start | bytes 786436
  27.4 10.3 %collective-permute-start.7 = (bf16[256,512]{1,0:T(8,128)(2,1)S(1)}, bf16[256,512]{1,0:T(8,128)(2,1)S(1)}, u32[]{:S(2)}, u32[]{:S(2)}) collective-permute-start(bf16[256,512]{1,0:T(8,128)(2,1)S(1)} %slice.21), channel_id=1, source_target_pairs={{0,6},{1,7},{2,0},{3,1},{4,2},{5,3},{6,4},{7,5},{8,14},{9,15},{10,... | collective-permute-start | bytes 786440 | tf_op jit(solution)/shard_map/ppermute | solution.py:36
  32.7 20.7 %collective-permute-start.8 = (bf16[512,512]{1,0:T(8,128)(2,1)S(1)}, bf16[512,512]{1,0:T(8,128)(2,1)S(1)}, u32[]{:S(2)}, u32[]{:S(2)}) collective-permute-start(bf16[512,512]{1,0:T(8,128)(2,1)S(1)} %collective-permute-done.2.refs_4_), channel_id=1, source_target_pairs={{0,8},{1,9},{2,10},{3,11},{4,12},{5,13},{6,14},{7,15},{8,16},{9,17... | collective-permute-start | bytes 1572872 | tf_op jit(solution)/shard_map/ppermute | solution.py:36
  35.8 12.3 %copy-start.7 = (bf16[256,512]{1,0:T(8,128)(2,1)}, bf16[256,512]{1,0:T(8,128)(2,1)S(1)}, u32[]{:S(2)}) copy-start(bf16[256,512]{1,0:T(8,128)(2,1)S(1)} %collective-permute-done.6.refs_3_) | copy-start | bytes 786436
  35.8 17.6 %collective-permute-start.9 = (bf16[512,512]{1,0:T(8,128)(2,1)S(1)}, bf16[512,512]{1,0:T(8,128)(2,1)S(1)}, u32[]{:S(2)}, u32[]{:S(2)}) collective-permute-start(bf16[512,512]{1,0:T(8,128)(2,1)S(1)} %collective-permute-done.3.refs_5_), channel_id=1, source_target_pairs={{0,24},{1,25},{2,26},{3,27},{4,28},{5,29},{6,30},{7,31},{8,0},{9,1... | collective-permute-start | bytes 1572872 | tf_op jit(solution)/shard_map/ppermute | solution.py:36
  37.7 10.4 %copy-start.8 = (bf16[256,512]{1,0:T(8,128)(2,1)}, bf16[256,512]{1,0:T(8,128)(2,1)S(1)}, u32[]{:S(2)}) copy-start(bf16[256,512]{1,0:T(8,128)(2,1)S(1)} %collective-permute-done.7.refs_4_) | copy-start | bytes 786436
  37.7 13.3 %collective-permute-start.10 = (bf16[256,512]{1,0:T(8,128)(2,1)S(1)}, bf16[256,512]{1,0:T(8,128)(2,1)S(1)}, u32[]{:S(2)}, u32[]{:S(2)}) collective-permute-start(bf16[256,512]{1,0:T(8,128)(2,1)S(1)} %collective-permute-done.6.refs_3_), channel_id=1, source_target_pairs={{0,8},{1,9},{2,10},{3,11},{4,12},{5,13},{6,14},{7,15},{8,16},{9,17... | collective-permute-start | bytes 786440 | tf_op jit(solution)/shard_map/ppermute | solution.py:36
  38.4 14.9 %collective-permute-start.11 = (bf16[256,512]{1,0:T(8,128)(2,1)S(1)}, bf16[256,512]{1,0:T(8,128)(2,1)S(1)}, u32[]{:S(2)}, u32[]{:S(2)}) collective-permute-start(bf16[256,512]{1,0:T(8,128)(2,1)S(1)} %collective-permute-done.7.refs_4_), channel_id=1, source_target_pairs={{0,24},{1,25},{2,26},{3,27},{4,28},{5,29},{6,30},{7,31},{8,0},{9,1... | collective-permute-start | bytes 786440 | tf_op jit(solution)/shard_map/ppermute | solution.py:36
  50.9 2.4 %copy-start.9 = (bf16[256,512]{1,0:T(8,128)(2,1)}, bf16[256,512]{1,0:T(8,128)(2,1)S(1)}, u32[]{:S(2)}) copy-start(bf16[256,512]{1,0:T(8,128)(2,1)S(1)} %collective-permute-done.10.refs_7_) | copy-start | bytes 786436
  53.3 0.7 copy-start.10
  53.3 0.9 copy-start.5
  53.4 1.0 copy-start.6
  118.4 5.0 %copy-start.1 = (bf16[4,512,512]{2,1,0:T(8,128)(2,1)S(1)}, bf16[4,512,512]{2,1,0:T(8,128)(2,1)}, u32[]{:S(2)}) copy-start(bf16[4,512,512]{2,1,0:T(8,128)(2,1)} %get-tuple-element.7.mine_a) | copy-start | bytes 6291460
  118.4 33.6 %copy-start.12 = (f32[1024,1,1,16]{0,3,2,1:T(8,128)S(1)}, f32[1024,1,1,16]{0,3,2,1:T(8,128)}, u32[]{:S(2)}) copy-start(f32[1024,1,1,16]{0,3,2,1:T(8,128)} %param.11) | copy-start | bytes 196612
  118.4 33.6 %copy-start.13 = (f32[1024,1,1,16]{0,3,2,1:T(8,128)S(1)}, f32[1024,1,1,16]{0,3,2,1:T(8,128)}, u32[]{:S(2)}) copy-start(f32[1024,1,1,16]{0,3,2,1:T(8,128)} %param.10) | copy-start | bytes 196612
  118.4 13.8 %all-to-all-start.1 = ((bf16[4,256,512]{2,1,0:T(8,128)(2,1)}), bf16[4,256,512]{2,1,0:T(8,128)(2,1)S(1)}, u32[]{:S(2)}, u32[]{:S(2)}) async-start(bf16[4,256,512]{2,1,0:T(8,128)(2,1)} %reduce_sum.33), calls=%async_computation.1 | async-start | bytes 2097152 | tf_op jit(solution)/shard_map/all_to_all | solution.py:56
  123.4 35.2 %collective-permute-start.13 = (bf16[4,512,512]{2,1,0:T(8,128)(2,1)}, bf16[4,512,512]{2,1,0:T(8,128)(2,1)}, u32[]{:S(2)}, u32[]{:S(2)}) collective-permute-start(bf16[4,512,512]{2,1,0:T(8,128)(2,1)} %get-tuple-element.9.mine_b), channel_id=1, source_target_pairs={{0,1},{1,0},{2,3},{3,2},{4,5},{5,4},{6,7},{7,6},{8,9},{9,8},{10,11... | collective-permute-start | bytes 6291464 | tf_op jit(solution)/shard_map/ppermute | solution.py:36
  123.4 35.2 %collective-permute-start.12 = (bf16[4,512,512]{2,1,0:T(8,128)(2,1)S(1)}, bf16[4,512,512]{2,1,0:T(8,128)(2,1)}, u32[]{:S(2)}, u32[]{:S(2)}) collective-permute-start(bf16[4,512,512]{2,1,0:T(8,128)(2,1)S(1)} %copy-done.1), channel_id=1, source_target_pairs={{0,1},{1,0},{2,3},{3,2},{4,5},{5,4},{6,7},{7,6},{8,9},{9,8},{10,11... | collective-permute-start | bytes 6291464 | tf_op jit(solution)/shard_map/ppermute | solution.py:36
  153.6 24.3 %all-to-all-start.3 = ((bf16[16,16,1024]{2,1,0:T(8,128)(2,1)}), bf16[16,16,1024]{2,1,0:T(8,128)(2,1)S(1)}, u32[]{:S(2)}, u32[]{:S(2)}) async-start(bf16[16,16,1024]{2,1,0:T(8,128)(2,1)} %broadcast_in_dim.2), calls=%async_computation.3 | async-start | bytes 1048576 | tf_op jit(solution)/shard_map/all_to_all | solution.py:323
  177.9 0.8 copy-start
